TPU v7x, 256 devices: a whole 4x4x8 slice. The times are simulated.
256 devices in a mesh: band: 64 (over z, x, core), tm: 4 (over y).
Axes of the slice: x: 4, y: 4, z: 8, core: 2. Of those that a mesh axis runs over, the one named last changes fastest.
Arguments:
- spectra: float32 [64, 64, 16384], P(None, 'band', 'tm'), may hold values from -6 to 6
- newest: float32 [64, 64, 4, 1024], P(None, 'band', 'tm')
- ingest_owner: int32 [64], P('band'), may hold values from 0 to 3
- low_trial: int32 [4, 4096], P(None, 'band'), may hold values from 0 to 7, as said below
- high_trial: int32 [4, 4096], P(None, 'band'), may hold values from 0 to 7, as said below
- delay_table: int32 [4, 4096], P(None, 'band'), may hold values from 0 to 64, as said below
Outputs:
- dedispersed: float32 [256, 16, 16384], P('band', None, 'tm')
Inputs may be any that keep to these rules, and one draw needn't show every extreme that they name: `low_trial`: at level l (row l-1) entry r belongs to trial r % 2^l and names a trial below 2^(l-1); the highest trial of each subband names trial 2^(l-1) - 1. `high_trial`: as low_trial, for the upper half-subband. `delay_table`: at level l the delays are at most 8 * 2^(l-1), reached by the highest trial of each subband.
All inputs are finite; a program needn't handle non-finite values.
Results may differ from a plain program's by a relative error of at most 0.0003.
Values sent between devices are 32-bit elements; how exact they have to be, the bound alone decides.
A program may use at most 64 MiB of HBM per device.

v0:
```python
import jax
import jax.numpy as jnp
from jax import lax
from jax.sharding import PartitionSpec as P

LEVELS = 4
SHIFT = 8


def spread(value, axis, source):
    kept = jnp.where(lax.axis_index(axis) == source, value, 0).astype(value.dtype)
    return lax.psum(kept, axis)


def from_behind(block, axis, distance):
    devices = range(lax.axis_size(axis))
    route = [(i - distance, i) for i in devices if i - distance in devices]
    return lax.ppermute(block, axis, route)


def channel_stats(ingest):
    block_mean = jnp.mean(ingest, axis=-1)
    centred = ingest - block_mean[:, None]
    inv_scale = 1.0 / jnp.sqrt(jnp.mean(centred * centred, axis=-1) + 1e-06)
    return (block_mean, inv_scale)


def delayed_rows(source, shifts, length):
    reach_max = source.shape[1] - length
    shifted = source
    for bit_pos in range(reach_max.bit_length()):
        step_size = 1 << bit_pos
        moved = jnp.concatenate(
            [jnp.zeros((source.shape[0], step_size), source.dtype), shifted[:, :-step_size]], axis=1
        )
        flags = jnp.right_shift(shifts, bit_pos) % 2 == 1
        shifted = jnp.where(flags[:, None], moved, shifted)
    return shifted[:, reach_max:]


def shards(spectra, newest, ingest_owner, low_trial, high_trial, delay_table):
    ingest = newest[:, 0, 0, :]
    root_slot = ingest_owner[0]
    received = spread(ingest, "tm", root_slot)
    block_mean, inv_scale = channel_stats(received)
    normed = (spectra[:, 0, :] - block_mean[:, None]) * inv_scale[:, None]
    chan_dev, time_dev = normed.shape
    moved = lax.all_to_all(
        normed[:, None, :], "band", split_axis=0, concat_axis=1, tiled=True
    ).reshape(chan_dev, time_dev)
    current = moved
    row_ids = jnp.arange(chan_dev, dtype=jnp.int32)
    for layer_idx in range(LEVELS):
        half_span = 2**layer_idx
        span_width = 2 * half_span
        reach_max = SHIFT * half_span
        low_rows = row_ids // span_width * span_width + low_trial[layer_idx]
        odd_rows = current.reshape(chan_dev // span_width, 2, half_span, time_dev)[:, 1].reshape(
            chan_dev // 2, time_dev
        )
        received_rim = from_behind(odd_rows[:, time_dev - reach_max :], "tm", 1)
        extended = jnp.concatenate([received_rim, odd_rows], axis=1)
        odd_index = row_ids // span_width * half_span + high_trial[layer_idx]
        current = current[low_rows] + delayed_rows(
            extended[odd_index], delay_table[layer_idx], time_dev
        )
    return current.reshape(chan_dev // 2**LEVELS, 2**LEVELS, time_dev)


def solution(mesh):
    return jax.shard_map(
        shards,
        mesh=mesh,
        in_specs=(
            P(None, "band", "tm"),
            P(None, "band", "tm", None),
            P("band"),
            P(None, "band"),
            P(None, "band"),
            P(None, "band"),
        ),
        out_specs=P("band", None, "tm"),
        check_vma=False,
    )
```

profile of v0, /device:TPU:16, one launch (start us, length us, event | category | flops | bytes accessed | tf_op | source)
XLA Modules:
  0.0 148.1 jit_solution(2413679411393339932)
XLA Ops:
  7.5 0.8 copy.18
  8.3 50.2 %all-reduce.24.cloned.1.call-done = f32[64,1024]{1,0:T(8,128)} async-done(((f32[64,1024]{1,0:T(8,128)}), f32[64,1024]{1,0:T(8,128)}) %all-reduce.24.cloned.1.call-update) | async-done | bytes 262160 | tf_op jit(solution)/shard_map/psum | solution.py:12
  58.5 1.1 reduce_sum.18
  59.6 1.2 multiply_reduce_fusion
  60.8 2.4 %subtract_multiply_fusion = f32[64,1,4096]{2,1,0:T(1,128)} fusion(f32[64,1,4096]{2,1,0:T(1,128)S(1)} %copy-done, f32[64]{0:T(128)S(1)} %add_rsqrt_fusion, f32[64]{0:T(128)S(1)} %broadcast_multiply_fusion), kind=kLoop, calls=%fused_computation.35 | loop fusion | flops 524288 | bytes 2097664 | tf_op jit(solution)/shard_map/mul | solution.py:46
  63.2 10.6 %all-to-all-start = ((f32[64,1,4096]{2,1,0:T(1,128)}), f32[64,1,4096]{2,1,0:T(1,128)S(1)}, u32[]{:S(2)}, u32[]{:S(2)}) async-start(f32[64,1,4096]{2,1,0:T(1,128)} %subtract_multiply_fusion), calls=%async_computation | async-start | bytes 2097152 | tf_op jit(solution)/shard_map/all_to_all | solution.py:48
  73.9 28.7 %all-to-all-done = f32[64,1,4096]{2,1,0:T(1,128)S(1)} async-done(((f32[64,1,4096]{2,1,0:T(1,128)}), f32[64,1,4096]{2,1,0:T(1,128)S(1)}, u32[]{:S(2)}, u32[]{:S(2)}) %all-to-all-start) | async-done | bytes 1048608 | tf_op jit(solution)/shard_map/all_to_all | solution.py:48
  103.1 2.8 %collective-permute-start = (f32[32,8]{1,0:T(8,128)S(1)}, f32[32,8]{1,0:T(8,128)S(1)}, u32[]{:S(2)}, u32[]{:S(2)}) collective-permute-start(f32[32,8]{1,0:T(8,128)S(1)} %slice.201), channel_id=1, source_target_pairs={{0,1},{1,2},{2,3},{4,5},{5,6},{6,7},{8,9},{9,10},{10,11},{12,13},{... | collective-permute-start | bytes 3080 | tf_op jit(solution)/shard_map/ppermute | solution.py:18
  106.5 0.9 gather_fusion
  107.4 1.3 collective-permute-done
  108.9 1.0 gather_fusion.1
  112.5 2.8 %collective-permute-start.1 = (f32[32,16]{1,0:T(8,128)S(1)}, f32[32,16]{1,0:T(8,128)S(1)}, u32[]{:S(2)}, u32[]{:S(2)}) collective-permute-start(f32[32,16]{1,0:T(8,128)S(1)} %slice.208), channel_id=1, source_target_pairs={{0,1},{1,2},{2,3},{4,5},{5,6},{6,7},{8,9},{9,10},{10,11},{12,13},{... | collective-permute-start | bytes 6152 | tf_op jit(solution)/shard_map/ppermute | solution.py:18
  115.3 0.9 gather_fusion.2
  116.2 1.9 %collective-permute-done.1 = f32[32,16]{1,0:T(8,128)S(1)} collective-permute-done((f32[32,16]{1,0:T(8,128)S(1)}, f32[32,16]{1,0:T(8,128)S(1)}, u32[]{:S(2)}, u32[]{:S(2)}) %collective-permute-start.1) | collective-permute-done | bytes 2080 | tf_op jit(solution)/shard_map/ppermute | solution.py:18
  118.3 1.0 gather_fusion.3
  121.8 3.0 %collective-permute-start.2 = (f32[32,32]{1,0:T(8,128)S(1)}, f32[32,32]{1,0:T(8,128)S(1)}, u32[]{:S(2)}, u32[]{:S(2)}) collective-permute-start(f32[32,32]{1,0:T(8,128)S(1)} %slice.216), channel_id=1, source_target_pairs={{0,1},{1,2},{2,3},{4,5},{5,6},{6,7},{8,9},{9,10},{10,11},{12,13},{... | collective-permute-start | bytes 12296 | tf_op jit(solution)/shard_map/ppermute | solution.py:18
  124.8 0.9 gather_fusion.4
  125.7 1.7 %collective-permute-done.2 = f32[32,32]{1,0:T(8,128)S(1)} collective-permute-done((f32[32,32]{1,0:T(8,128)S(1)}, f32[32,32]{1,0:T(8,128)S(1)}, u32[]{:S(2)}, u32[]{:S(2)}) %collective-permute-start.2) | collective-permute-done | bytes 4128 | tf_op jit(solution)/shard_map/ppermute | solution.py:18
  127.6 1.0 gather_fusion.5
  130.9 2.8 %collective-permute-start.3 = (f32[32,64]{1,0:T(8,128)S(1)}, f32[32,64]{1,0:T(8,128)S(1)}, u32[]{:S(2)}, u32[]{:S(2)}) collective-permute-start(f32[32,64]{1,0:T(8,128)S(1)} %slice.225), channel_id=1, source_target_pairs={{0,1},{1,2},{2,3},{4,5},{5,6},{6,7},{8,9},{9,10},{10,11},{12,13},{... | collective-permute-start | bytes 24584 | tf_op jit(solution)/shard_map/ppermute | solution.py:18
  133.7 0.9 gather_fusion.6
  134.7 1.9 %collective-permute-done.3 = f32[32,64]{1,0:T(8,128)S(1)} collective-permute-done((f32[32,64]{1,0:T(8,128)S(1)}, f32[32,64]{1,0:T(8,128)S(1)}, u32[]{:S(2)}, u32[]{:S(2)}) %collective-permute-start.3) | collective-permute-done | bytes 8224 | tf_op jit(solution)/shard_map/ppermute | solution.py:18
  136.7 1.0 gather_fusion.7
  139.9 1.3 fusion
  (67 shorter events, 11.7 us)
Async XLA Ops:
  6.5 54.2 %copy-start = (f32[64,1,4096]{2,1,0:T(1,128)S(1)}, f32[64,1,4096]{2,1,0:T(1,128)}, u32[]{:S(2)}) copy-start(f32[64,1,4096]{2,1,0:T(1,128)} %param.6) | copy-start | bytes 3145732
  6.5 52.0 %all-reduce.24.cloned.1.call-start = ((), (), s32[]{:S(2)}) async-start(), calls=%async_computation.1 | async-start | bytes 524288 | tf_op jit(solution)/shard_map/psum | solution.py:12
  63.2 10.6 %copy-start.2 = (s32[4,64]{1,0:T(4,128)S(1)}, s32[4,64]{1,0:T(4,128)}, u32[]{:S(2)}) copy-start(s32[4,64]{1,0:T(4,128)} %param.9) | copy-start | bytes 3076
  63.2 10.6 %copy-start.3 = (s32[4,64]{1,0:T(4,128)S(1)}, s32[4,64]{1,0:T(4,128)}, u32[]{:S(2)}) copy-start(s32[4,64]{1,0:T(4,128)} %param.10) | copy-start | bytes 3076
  63.2 10.7 %copy-start.1 = (s32[4,64]{1,0:T(4,128)S(1)}, s32[4,64]{1,0:T(4,128)}, u32[]{:S(2)}) copy-start(s32[4,64]{1,0:T(4,128)} %param.11) | copy-start | bytes 3076
  63.2 39.5 %all-to-all-start = ((f32[64,1,4096]{2,1,0:T(1,128)}), f32[64,1,4096]{2,1,0:T(1,128)S(1)}, u32[]{:S(2)}, u32[]{:S(2)}) async-start(f32[64,1,4096]{2,1,0:T(1,128)} %subtract_multiply_fusion), calls=%async_computation | async-start | bytes 2097152 | tf_op jit(solution)/shard_map/all_to_all | solution.py:48
  103.1 5.6 %collective-permute-start = (f32[32,8]{1,0:T(8,128)S(1)}, f32[32,8]{1,0:T(8,128)S(1)}, u32[]{:S(2)}, u32[]{:S(2)}) collective-permute-start(f32[32,8]{1,0:T(8,128)S(1)} %slice.201), channel_id=1, source_target_pairs={{0,1},{1,2},{2,3},{4,5},{5,6},{6,7},{8,9},{9,10},{10,11},{12,13},{... | collective-permute-start | bytes 3080 | tf_op jit(solution)/shard_map/ppermute | solution.py:18
  112.5 5.6 %collective-permute-start.1 = (f32[32,16]{1,0:T(8,128)S(1)}, f32[32,16]{1,0:T(8,128)S(1)}, u32[]{:S(2)}, u32[]{:S(2)}) collective-permute-start(f32[32,16]{1,0:T(8,128)S(1)} %slice.208), channel_id=1, source_target_pairs={{0,1},{1,2},{2,3},{4,5},{5,6},{6,7},{8,9},{9,10},{10,11},{12,13},{... | collective-permute-start | bytes 6152 | tf_op jit(solution)/shard_map/ppermute | solution.py:18
  121.8 5.6 %collective-permute-start.2 = (f32[32,32]{1,0:T(8,128)S(1)}, f32[32,32]{1,0:T(8,128)S(1)}, u32[]{:S(2)}, u32[]{:S(2)}) collective-permute-start(f32[32,32]{1,0:T(8,128)S(1)} %slice.216), channel_id=1, source_target_pairs={{0,1},{1,2},{2,3},{4,5},{5,6},{6,7},{8,9},{9,10},{10,11},{12,13},{... | collective-permute-start | bytes 12296 | tf_op jit(solution)/shard_map/ppermute | solution.py:18
  130.9 5.6 %collective-permute-start.3 = (f32[32,64]{1,0:T(8,128)S(1)}, f32[32,64]{1,0:T(8,128)S(1)}, u32[]{:S(2)}, u32[]{:S(2)}) collective-permute-start(f32[32,64]{1,0:T(8,128)S(1)} %slice.225), channel_id=1, source_target_pairs={{0,1},{1,2},{2,3},{4,5},{5,6},{6,7},{8,9},{9,10},{10,11},{12,13},{... | collective-permute-start | bytes 24584 | tf_op jit(solution)/shard_map/ppermute | solution.py:18
Sparse Core Ops, SparseCore 0:
  9.7 48.7 all-reduce.23
where the time goes:
time: 148 us
  waiting for transfers between devices  85.7 us (58%)
  starting transfers between devices  21.9 us (15%)
  between operations  14.6 us (10%)
  other arithmetic  14.5 us (10%)
  local copies, waits for them, and re-layouts  11.5 us (8%)
    psum x1, waiting for transfers between devices, spread(): return lax.psum(kept, axis)  50.2 us
    all_to_all x1, waiting for transfers between devices, shards(): lax.all_to_all(normed[:, None, :], 'band', split_axis=0, concat_axis=1, t...  28.7 us
    ppermute x4, starting transfers between devices, from_behind(): return lax.ppermute(block, axis, route)  11.3 us
    all_to_all x1, starting transfers between devices, shards(): lax.all_to_all(normed[:, None, :], 'band', split_axis=0, concat_axis=1, t...  10.6 us
    ppermute x4, waiting for transfers between devices, from_behind(): return lax.ppermute(block, axis, route)  6.74 us
    select_n x18, other arithmetic, delayed_rows(): shifted = jnp.where(flags[:, None], moved, shifted)  6.34 us
    gather x4, local copies, waits for them, and re-layouts, shards(): extended[odd_index]  3.88 us
    gather x4, local copies, waits for them, and re-layouts, shards(): current[low_rows]  3.7 us
  transfers between devices with their start and end apart: 6, of which 6 were waited for; matrix products, arithmetic and copies ran while one was open for 3% of the time, Pallas kernels for 0%

commit v1 on v0

--- a/solution.py
+++ b/solution.py
@@ -9,7 +9,7 @@
 
 def spread(value, axis, source):
     kept = jnp.where(lax.axis_index(axis) == source, value, 0).astype(value.dtype)
-    return lax.psum(kept, axis)
+    return jnp.sum(lax.all_gather(kept, axis), axis=0)
 
 
 def from_behind(block, axis, distance):

time: 148 us -> 130 us (0.88)
  waiting for transfers between devices: 85.7 us -> 63.8 us
  local copies, waits for them, and re-layouts: 11.5 us -> 13.3 us
    psum x1 -> x0, waiting for transfers between devices: 50.2 us -> none  [spread(): return lax.psum(kept, axis)]
    all_gather x0 -> x1, waiting for transfers between devices: none -> 29.5 us  [spread(): return jnp.sum(lax.all_gather(kept, axis), axis=0)]
    unnamed x11 -> x13, local copies, waits for them, and re-layouts: 1.68 us -> 3.48 us
where the time goes in v1:
time: 130 us; the launch traced here: 129 us
  waiting for transfers between devices  63.8 us (49%)
  starting transfers between devices  23 us (18%)
  between operations  14.5 us (11%)
  other arithmetic  14.4 us (11%)
  local copies, waits for them, and re-layouts  13.3 us (10%)
    all_gather x1, waiting for transfers between devices, spread(): return jnp.sum(lax.all_gather(kept, axis), axis=0)  29.5 us
    all_to_all x1, waiting for transfers between devices, shards(): lax.all_to_all(normed[:, None, :], 'band', split_axis=0, concat_axis=1, t...  28.7 us
    ppermute x4, starting transfers between devices, from_behind(): return lax.ppermute(block, axis, route)  12.5 us
    all_to_all x1, starting transfers between devices, shards(): lax.all_to_all(normed[:, None, :], 'band', split_axis=0, concat_axis=1, t...  10.6 us
    select_n x18, other arithmetic, delayed_rows(): shifted = jnp.where(flags[:, None], moved, shifted)  6.34 us
    ppermute x4, waiting for transfers between devices, from_behind(): return lax.ppermute(block, axis, route)  5.58 us
    gather x4, local copies, waits for them, and re-layouts, shards(): extended[odd_index]  3.88 us
    gather x4, local copies, waits for them, and re-layouts, shards(): current[low_rows]  3.7 us
  transfers between devices with their start and end apart: 6, of which 6 were waited for; matrix products, arithmetic and copies ran while one was open for 3% of the time, Pallas kernels for 0%

profile of v1, /device:TPU:16, one launch (start us, length us, event | category | flops | bytes accessed | tf_op | source)
XLA Modules:
  0.0 129.0 jit_solution(1689201676267720752)
XLA Ops:
  7.2 0.9 broadcast_select_fusion
  8.2 29.5 %all-gather.3.cloned.1.call-done = f32[256,1,1,1024]{3,2,1,0:T(1,128)} async-done(((f32[64,1,1,1024]{3,2,1,0:T(1,128)}), f32[256,1,1,1024]{3,2,1,0:T(1,128)}) %all-gather.3.cloned.1.call-update) | async-done | bytes 1048592 | tf_op jit(solution)/shard_map/all_gather | solution.py:12
  37.6 1.4 %copy.11 = f32[256,1,1,1024]{3,0,1,2:T(8,128)S(1)} copy(f32[256,1,1,1024]{3,2,1,0:T(1,128)} %all-gather.3.cloned.1.call-done) | data formatting | bytes 2097152
  39.2 1.1 copy-done
  40.3 1.1 reduce.1
  41.7 2.4 %subtract_multiply_fusion = f32[64,1,4096]{2,1,0:T(1,128)} fusion(f32[64,1,4096]{2,1,0:T(1,128)S(1)} %copy-done.1, f32[64]{0:T(128)S(1)} %add_rsqrt_fusion, f32[64]{0:T(128)S(1)} %broadcast_multiply_fusion), kind=kLoop, calls=%fused_computation.35 | loop fusion | flops 524288 | bytes 2097664 | tf_op jit(solution)/shard_map/mul | solution.py:46
  44.1 10.6 %all-to-all-start = ((f32[64,1,4096]{2,1,0:T(1,128)}), f32[64,1,4096]{2,1,0:T(1,128)S(1)}, u32[]{:S(2)}, u32[]{:S(2)}) async-start(f32[64,1,4096]{2,1,0:T(1,128)} %subtract_multiply_fusion), calls=%async_computation | async-start | bytes 2097152 | tf_op jit(solution)/shard_map/all_to_all | solution.py:48
  54.9 28.7 %all-to-all-done = f32[64,1,4096]{2,1,0:T(1,128)S(1)} async-done(((f32[64,1,4096]{2,1,0:T(1,128)}), f32[64,1,4096]{2,1,0:T(1,128)S(1)}, u32[]{:S(2)}, u32[]{:S(2)}) %all-to-all-start) | async-done | bytes 1048608 | tf_op jit(solution)/shard_map/all_to_all | solution.py:48
  84.0 3.1 %collective-permute-start = (f32[32,8]{1,0:T(8,128)S(1)}, f32[32,8]{1,0:T(8,128)S(1)}, u32[]{:S(2)}, u32[]{:S(2)}) collective-permute-start(f32[32,8]{1,0:T(8,128)S(1)} %slice.201), channel_id=1, source_target_pairs={{0,1},{1,2},{2,3},{4,5},{5,6},{6,7},{8,9},{9,10},{10,11},{12,13},{... | collective-permute-start | bytes 3080 | tf_op jit(solution)/shard_map/ppermute | solution.py:18
  88.6 1.0 collective-permute-done
  89.8 1.0 gather_fusion.1
  93.4 3.3 %collective-permute-start.1 = (f32[32,16]{1,0:T(8,128)S(1)}, f32[32,16]{1,0:T(8,128)S(1)}, u32[]{:S(2)}, u32[]{:S(2)}) collective-permute-start(f32[32,16]{1,0:T(8,128)S(1)} %slice.208), channel_id=1, source_target_pairs={{0,1},{1,2},{2,3},{4,5},{5,6},{6,7},{8,9},{9,10},{10,11},{12,13},{... | collective-permute-start | bytes 6152 | tf_op jit(solution)/shard_map/ppermute | solution.py:18
  96.7 0.9 gather_fusion.2
  97.6 1.4 %collective-permute-done.1 = f32[32,16]{1,0:T(8,128)S(1)} collective-permute-done((f32[32,16]{1,0:T(8,128)S(1)}, f32[32,16]{1,0:T(8,128)S(1)}, u32[]{:S(2)}, u32[]{:S(2)}) %collective-permute-start.1) | collective-permute-done | bytes 2080 | tf_op jit(solution)/shard_map/ppermute | solution.py:18
  99.3 1.0 gather_fusion.3
  102.7 3.1 %collective-permute-start.2 = (f32[32,32]{1,0:T(8,128)S(1)}, f32[32,32]{1,0:T(8,128)S(1)}, u32[]{:S(2)}, u32[]{:S(2)}) collective-permute-start(f32[32,32]{1,0:T(8,128)S(1)} %slice.216), channel_id=1, source_target_pairs={{0,1},{1,2},{2,3},{4,5},{5,6},{6,7},{8,9},{9,10},{10,11},{12,13},{... | collective-permute-start | bytes 12296 | tf_op jit(solution)/shard_map/ppermute | solution.py:18
  105.8 0.9 gather_fusion.4
  106.7 1.6 %collective-permute-done.2 = f32[32,32]{1,0:T(8,128)S(1)} collective-permute-done((f32[32,32]{1,0:T(8,128)S(1)}, f32[32,32]{1,0:T(8,128)S(1)}, u32[]{:S(2)}, u32[]{:S(2)}) %collective-permute-start.2) | collective-permute-done | bytes 4128 | tf_op jit(solution)/shard_map/ppermute | solution.py:18
  108.5 1.0 gather_fusion.5
  111.9 3.1 %collective-permute-start.3 = (f32[32,64]{1,0:T(8,128)S(1)}, f32[32,64]{1,0:T(8,128)S(1)}, u32[]{:S(2)}, u32[]{:S(2)}) collective-permute-start(f32[32,64]{1,0:T(8,128)S(1)} %slice.225), channel_id=1, source_target_pairs={{0,1},{1,2},{2,3},{4,5},{5,6},{6,7},{8,9},{9,10},{10,11},{12,13},{... | collective-permute-start | bytes 24584 | tf_op jit(solution)/shard_map/ppermute | solution.py:18
  114.9 0.9 gather_fusion.6
  115.9 1.6 %collective-permute-done.3 = f32[32,64]{1,0:T(8,128)S(1)} collective-permute-done((f32[32,64]{1,0:T(8,128)S(1)}, f32[32,64]{1,0:T(8,128)S(1)}, u32[]{:S(2)}, u32[]{:S(2)}) %collective-permute-start.3) | collective-permute-done | bytes 8224 | tf_op jit(solution)/shard_map/ppermute | solution.py:18
  117.7 1.0 gather_fusion.7
  120.9 1.3 %fusion = f32[64,4096]{1,0:T(8,128)} fusion(f32[64,4096]{1,0:T(8,128)S(1)} %gather_fusion.6, f32[64,4160]{1,0:T(8,128)S(1)} %pad_select_fusion, f32[64,4096]{1,0:T(8,128)S(1)} %slice.232, pred[64]{0:T(512)(128)(4,1)S(1)} %get-tuple-element.5), kind=kLoop, calls=%fused_computation.27 | loop fusion | flops 524288 | bytes 4194368 | tf_op jit(solution)/shard_map/add | solution.py:64
  (72 shorter events, 12.8 us)
Async XLA Ops:
  6.5 31.1 %all-gather.3.cloned.1.call-start = ((), (), s32[]{:S(2)}) async-start(), calls=%async_computation.1 | async-start | bytes 1310720 | tf_op jit(solution)/shard_map/all_gather | solution.py:12
  39.1 1.2 copy-start
  39.1 2.6 %copy-start.1 = (f32[64,1,4096]{2,1,0:T(1,128)S(1)}, f32[64,1,4096]{2,1,0:T(1,128)}, u32[]{:S(2)}) copy-start(f32[64,1,4096]{2,1,0:T(1,128)} %param.6) | copy-start | bytes 3145732
  44.1 10.6 %copy-start.3 = (s32[4,64]{1,0:T(4,128)S(1)}, s32[4,64]{1,0:T(4,128)}, u32[]{:S(2)}) copy-start(s32[4,64]{1,0:T(4,128)} %param.9) | copy-start | bytes 3076
  44.1 10.6 %copy-start.4 = (s32[4,64]{1,0:T(4,128)S(1)}, s32[4,64]{1,0:T(4,128)}, u32[]{:S(2)}) copy-start(s32[4,64]{1,0:T(4,128)} %param.10) | copy-start | bytes 3076
  44.1 10.7 %copy-start.2 = (s32[4,64]{1,0:T(4,128)S(1)}, s32[4,64]{1,0:T(4,128)}, u32[]{:S(2)}) copy-start(s32[4,64]{1,0:T(4,128)} %param.11) | copy-start | bytes 3076
  44.1 39.5 %all-to-all-start = ((f32[64,1,4096]{2,1,0:T(1,128)}), f32[64,1,4096]{2,1,0:T(1,128)S(1)}, u32[]{:S(2)}, u32[]{:S(2)}) async-start(f32[64,1,4096]{2,1,0:T(1,128)} %subtract_multiply_fusion), calls=%async_computation | async-start | bytes 2097152 | tf_op jit(solution)/shard_map/all_to_all | solution.py:48
  84.0 5.6 %collective-permute-start = (f32[32,8]{1,0:T(8,128)S(1)}, f32[32,8]{1,0:T(8,128)S(1)}, u32[]{:S(2)}, u32[]{:S(2)}) collective-permute-start(f32[32,8]{1,0:T(8,128)S(1)} %slice.201), channel_id=1, source_target_pairs={{0,1},{1,2},{2,3},{4,5},{5,6},{6,7},{8,9},{9,10},{10,11},{12,13},{... | collective-permute-start | bytes 3080 | tf_op jit(solution)/shard_map/ppermute | solution.py:18
  93.4 5.6 %collective-permute-start.1 = (f32[32,16]{1,0:T(8,128)S(1)}, f32[32,16]{1,0:T(8,128)S(1)}, u32[]{:S(2)}, u32[]{:S(2)}) collective-permute-start(f32[32,16]{1,0:T(8,128)S(1)} %slice.208), channel_id=1, source_target_pairs={{0,1},{1,2},{2,3},{4,5},{5,6},{6,7},{8,9},{9,10},{10,11},{12,13},{... | collective-permute-start | bytes 6152 | tf_op jit(solution)/shard_map/ppermute | solution.py:18
  102.7 5.6 %collective-permute-start.2 = (f32[32,32]{1,0:T(8,128)S(1)}, f32[32,32]{1,0:T(8,128)S(1)}, u32[]{:S(2)}, u32[]{:S(2)}) collective-permute-start(f32[32,32]{1,0:T(8,128)S(1)} %slice.216), channel_id=1, source_target_pairs={{0,1},{1,2},{2,3},{4,5},{5,6},{6,7},{8,9},{9,10},{10,11},{12,13},{... | collective-permute-start | bytes 12296 | tf_op jit(solution)/shard_map/ppermute | solution.py:18
  111.9 5.6 %collective-permute-start.3 = (f32[32,64]{1,0:T(8,128)S(1)}, f32[32,64]{1,0:T(8,128)S(1)}, u32[]{:S(2)}, u32[]{:S(2)}) collective-permute-start(f32[32,64]{1,0:T(8,128)S(1)} %slice.225), channel_id=1, source_target_pairs={{0,1},{1,2},{2,3},{4,5},{5,6},{6,7},{8,9},{9,10},{10,11},{12,13},{... | collective-permute-start | bytes 24584 | tf_op jit(solution)/shard_map/ppermute | solution.py:18
Sparse Core Ops, SparseCore 0:
  9.2 28.4 all-gather.2
